TPU v7x, 128 devices: a whole 4x4x4 slice. The times are simulated.
128 devices in a mesh: seg: 8 (over z, core), sec: 16 (over x, y).
Axes of the slice: x: 4, y: 4, z: 4, core: 2. Of those that a mesh axis runs over, the one named last changes fastest.
Arguments:
- wave_first: float32 [8, 128, 128, 128], P('seg', 'sec')
- wave_second: float32 [8, 128, 128, 128], P('seg', 'sec')
- onsite_first: float32 [8, 128, 128, 128], P('seg', 'sec'), may hold values from 0.5 to 4
- onsite_second: float32 [8, 128, 128, 128], P('seg', 'sec'), may hold values from 0.5 to 4
- left_first: bfloat16 [8, 128, 16, 128, 128], P('seg', 'sec'), may hold values from -0.5 to 0.5
- right_first: bfloat16 [8, 128, 16, 128, 128], P('seg', 'sec'), may hold values from -0.125 to 0.125
- left_base: bfloat16 [8, 128, 16, 128, 128], P('seg', 'sec'), may hold values from -0.5 to 0.5
- right_second: bfloat16 [8, 128, 16, 128, 128], P('seg', 'sec'), may hold values from -0.125 to 0.125
- sources: int32 [128, 16], P('sec'), may hold values from 0 to 127, as said below
- block_dims: int32 [128], P('sec'), may hold values from 8 to 128, as said below
Outputs:
- result_first: float32 [8, 128, 128, 128], P('seg', 'sec')
- result_second: float32 [8, 128, 128, 128], P('seg', 'sec')
Inputs may be any that keep to these rules, and one draw needn't show every extreme that they name: `sources`: each entry names a block whose index differs from its row's block by at most 8, and that difference is reached. `block_dims`: a multiple of 8.
All inputs are finite; a program needn't handle non-finite values.
Results may differ from a plain program's by a relative error of at most 0.015.
Values may be sent and summed in bfloat16 or wider, within the bound.
A program may use at most 128 MiB of HBM per device.

v0:
```python
import jax
import jax.numpy as jnp
from jax import lax
from jax.sharding import PartitionSpec as P

STEPS = 3


def extended_2(block, sides, width):
    for axis, dim in sides:
        count = lax.axis_size(axis)
        forward = [(i, i + 1) for i in range(count - 1)]
        backward = [(target, source) for source, target in forward]
        low = lax.ppermute(
            lax.slice_in_dim(block, block.shape[dim] - width, None, axis=dim), axis, forward
        )
        high = lax.ppermute(lax.slice_in_dim(block, 0, width, axis=dim), axis, backward)
        block = jnp.concatenate([low, block, high], axis=dim)
    return block


def passed_along(value, axis, steps):
    count = lax.axis_size(axis)
    initial, last = (max(0, -steps), min(count, count - steps))
    return lax.ppermute(value, axis, [(source, source + steps) for source in range(initial, last)])


def live_mask(block_dims, tile_width):
    row_index = lax.broadcasted_iota(jnp.int32, (block_dims.shape[0], tile_width, tile_width), 1)
    col_index = lax.broadcasted_iota(jnp.int32, (block_dims.shape[0], tile_width, tile_width), 2)
    limit = block_dims[:, None, None]
    return ((row_index < limit) & (col_index < limit)).astype(jnp.float32)


def operate(vector, onsite, live, left_env, right_env, local_source):
    packed = vector.astype(jnp.bfloat16)
    extended = extended_2(packed, (("sec", 1),), packed.shape[1])
    picked = jnp.take(extended[0], local_source, axis=0)
    left_part = jnp.einsum(
        "bkij,bkjl->bkil", left_env[0], picked, preferred_element_type=jnp.float32
    ).astype(jnp.bfloat16)
    terms = jnp.einsum(
        "bkil,bklm->bim", left_part, right_env[0], preferred_element_type=jnp.float32
    )
    return live * (onsite * vector + terms[None])


def davidson(start, onsite, left_env, right_env, live, local_source, entries):
    vector = live * start
    for iteration in range(STEPS):
        image = operate(vector, onsite, live, left_env, right_env, local_source)
        cross, square = lax.psum((jnp.sum(vector * image), jnp.sum(vector * vector)), "sec")
        quotient = cross / square
        moved = vector - (image - quotient * vector) / (onsite + 1.0)
        length = lax.psum(jnp.sum(moved * moved), "sec")
        vector = moved / jnp.sqrt(length / entries + 1e-06)
    return vector


def on_device(
    wave_first,
    wave_second,
    onsite_first,
    onsite_second,
    left_first,
    right_first,
    left_base,
    right_second,
    sources,
    block_dims,
):
    tile_width = wave_first.shape[2]
    block_count = wave_first.shape[1]
    entries = block_count * lax.axis_size("sec") * tile_width * tile_width
    live = live_mask(block_dims, tile_width)[None]
    local_source = sources - lax.axis_index("sec") * block_count + block_count
    result_first = davidson(
        wave_first, onsite_first, left_first, right_first, live, local_source, entries
    )
    handed = passed_along(result_first.astype(jnp.bfloat16), "seg", 1)
    carried = jnp.einsum(
        "sbkij,sbjl->sbkil", left_base, handed, preferred_element_type=jnp.float32
    ).astype(jnp.bfloat16)
    added = jnp.einsum("sbji,sbkjl->sbkil", handed, carried, preferred_element_type=jnp.float32)
    left_second = (left_base.astype(jnp.float32) + added / tile_width).astype(jnp.bfloat16)
    result_second = davidson(
        wave_second, onsite_second, left_second, right_second, live, local_source, entries
    )
    return (result_first, result_second)


def solution(mesh):
    placed = (
        P("seg", "sec", None, None),
        P("seg", "sec", None, None),
        P("seg", "sec", None, None),
        P("seg", "sec", None, None),
        P("seg", "sec", None, None, None),
        P("seg", "sec", None, None, None),
        P("seg", "sec", None, None, None),
        P("seg", "sec", None, None, None),
        P("sec", None),
        P("sec"),
    )
    return jax.shard_map(
        on_device,
        mesh=mesh,
        in_specs=placed,
        out_specs=(P("seg", "sec", None, None), P("seg", "sec", None, None)),
        check_vma=False,
    )
```

profile of v0, /device:TPU:32, one launch (start us, length us, event | category | flops | bytes accessed | tf_op | source)
XLA Modules:
  0.0 606.9 jit_solution(15143702878233935539)
XLA Ops:
  3.4 4.6 collective-permute-start
  8.7 3.3 collective-permute-done.1
  13.3 3.0 gather_fusion
  16.3 7.7 %multiply_reduce_fusion.16 = (f32[]{:T(128)}, f32[]{:T(128)}, f32[1,8,128,128]{3,2,1,0:T(8,128)S(1)}) fusion(f32[1,8,128,128]{3,2,1,0:T(8,128)S(1)} %copy-done.2, s32[8]{0:T(128)S(1)} %copy-done.4, bf16[1,8,16,128,128]{4,3,2,1,0:T(8,128)(2,1)} %param.17, bf16[8,16,128,128]{3,2,1,0:T(8,128)(2,1)} %bitcast.240, pred[8,16]{1,0:T(8,128)(4,1)S(1)} %get-tuple-element.41, ...), kind=kOutput, calls=%fused_computation.108 | convolution fusion | flops 1079377920 | bytes 14155944 | tf_op jit(solution)/shard_map/bkil,bklm->bim/dot_general | solution.py:42
  24.0 42.5 %all-reduce.5 = (f32[]{:T(128)}, f32[]{:T(128)}) all-reduce(f32[]{:T(128)} %get-tuple-element.6, f32[]{:T(128)} %get-tuple-element.5), channel_id=1, replica_groups=mesh['seg'=8,'sec'=16] {'sec'}, use_global_device_ids=true, to_apply=%region_1.3 | all-reduce | flops 2 | bytes 16 | tf_op jit(solution)/shard_map/psum | solution.py:52
  68.7 36.1 %psum.128 = f32[]{:T(128)} all-reduce(f32[]{:T(128)} %get-tuple-element.39), channel_id=1, replica_groups=mesh['seg'=8,'sec'=16] {'sec'}, use_global_device_ids=true, to_apply=%region_5.7 | all-reduce | flops 1 | bytes 8 | tf_op jit(solution)/shard_map/psum | solution.py:55
  106.9 4.6 collective-permute-start.2
  115.4 3.0 gather_fusion.1
  118.4 7.7 %multiply_reduce_fusion.13 = (f32[]{:T(128)}, f32[]{:T(128)}, f32[1,8,128,128]{3,2,1,0:T(8,128)S(1)}) fusion(f32[1,8,128,128]{3,2,1,0:T(8,128)S(1)} %get-tuple-element.40, f32[]{:T(128)S(6)} %sqrt.18, bf16[1,8,16,128,128]{4,3,2,1,0:T(8,128)(2,1)} %param.17, bf16[8,16,128,128]{3,2,1,0:T(8,128)(2,1)} %bitcast.241, pred[8,16]{1,0:T(8,128)(4,1)S(1)} %get-tuple-element.41, ...), kind=kOutput, calls=%fused_computation.104 | convolution fusion | flops 1079377920 | bytes 14155948 | tf_op jit(solution)/shard_map/bkil,bklm->bim/dot_general | solution.py:42
  126.1 38.6 %all-reduce.4 = (f32[]{:T(128)}, f32[]{:T(128)}) all-reduce(f32[]{:T(128)} %get-tuple-element.14, f32[]{:T(128)} %get-tuple-element.13), channel_id=1, replica_groups=mesh['seg'=8,'sec'=16] {'sec'}, use_global_device_ids=true, to_apply=%region_7.9 | all-reduce | flops 2 | bytes 16 | tf_op jit(solution)/shard_map/psum | solution.py:52
  166.8 36.1 %psum.131 = f32[]{:T(128)} all-reduce(f32[]{:T(128)} %get-tuple-element.37), channel_id=1, replica_groups=mesh['seg'=8,'sec'=16] {'sec'}, use_global_device_ids=true, to_apply=%region_11.13 | all-reduce | flops 1 | bytes 8 | tf_op jit(solution)/shard_map/psum | solution.py:55
  204.9 4.6 collective-permute-start.4
  210.8 4.6 collective-permute-start.7
  215.5 3.0 gather_fusion.2
  218.5 7.7 %multiply_reduce_fusion.10 = (f32[]{:T(128)}, f32[]{:T(128)}, f32[1,8,128,128]{3,2,1,0:T(8,128)S(1)}) fusion(f32[1,8,128,128]{3,2,1,0:T(8,128)S(1)} %get-tuple-element.38, f32[]{:T(128)S(6)} %sqrt.19, bf16[1,8,16,128,128]{4,3,2,1,0:T(8,128)(2,1)} %param.17, bf16[8,16,128,128]{3,2,1,0:T(8,128)(2,1)} %bitcast.242, pred[8,16]{1,0:T(8,128)(4,1)S(1)} %get-tuple-element.41, ...), kind=kOutput, calls=%fused_computation.100 | convolution fusion | flops 1079377920 | bytes 14155948 | tf_op jit(solution)/shard_map/bkil,bklm->bim/dot_general | solution.py:42
  226.2 38.1 %all-reduce.3 = (f32[]{:T(128)}, f32[]{:T(128)}) all-reduce(f32[]{:T(128)} %get-tuple-element.12, f32[]{:T(128)} %get-tuple-element.11), channel_id=1, replica_groups=mesh['seg'=8,'sec'=16] {'sec'}, use_global_device_ids=true, to_apply=%region_13.15 | all-reduce | flops 2 | bytes 16 | tf_op jit(solution)/shard_map/psum | solution.py:52
  266.4 36.3 %psum.134 = f32[]{:T(128)} all-reduce(f32[]{:T(128)} %get-tuple-element.35), channel_id=1, replica_groups=mesh['seg'=8,'sec'=16] {'sec'}, use_global_device_ids=true, to_apply=%region_17.19 | all-reduce | flops 1 | bytes 8 | tf_op jit(solution)/shard_map/psum | solution.py:55
  306.1 6.5 %copy.12 = bf16[1,8,16,128,128]{3,4,2,1,0:T(8,128)(2,1)} copy(bf16[1,8,16,128,128]{4,3,2,1,0:T(8,128)(2,1)} %param.18) | data formatting | bytes 8388608 | tf_op args[6]
  312.7 3.0 gather_fusion.3
  315.7 8.0 %fusion.1 = bf16[8,16,128,128]{2,3,1,0:T(8,128)(2,1)} fusion(bf16[1,8,16,128,128]{3,4,2,1,0:T(8,128)(2,1)} %copy.12, bf16[1,8,16,128,128]{4,3,2,1,0:T(8,128)(2,1)} %param.18, bf16[1,8,128,128]{3,2,1,0:T(8,128)(2,1)S(1)} %collective-permute-done.6), kind=kOutput, calls=%fused_computation.8 | convolution fusion | flops 1084227584 | bytes 12845056 | tf_op jit(solution)/shard_map/sbji,sbkjl->sbkil/dot_general | solution.py:84
  323.8 8.1 %multiply_reduce_fusion.7 = (f32[]{:T(128)}, f32[]{:T(128)}, f32[1,8,128,128]{3,2,1,0:T(8,128)S(1)}) fusion(f32[1,8,128,128]{3,2,1,0:T(8,128)S(1)} %copy-done.3, s32[8]{0:T(128)S(1)} %copy-done.4, bf16[1,8,16,128,128]{4,3,2,1,0:T(8,128)(2,1)} %param.19, bf16[8,16,128,128]{2,3,1,0:T(8,128)(2,1)} %fusion.1, bf16[8,16,128,128]{3,2,1,0:T(8,128)(2,1)} %bitcast.238, ...), kind=kOutput, calls=%fused_computation.96 | convolution fusion | flops 1079377920 | bytes 14155944 | tf_op jit(solution)/shard_map/bkil,bklm->bim/dot_general | solution.py:42
  331.8 38.2 %all-reduce.2 = (f32[]{:T(128)}, f32[]{:T(128)}) all-reduce(f32[]{:T(128)} %get-tuple-element.4, f32[]{:T(128)} %get-tuple-element.3), channel_id=1, replica_groups=mesh['seg'=8,'sec'=16] {'sec'}, use_global_device_ids=true, to_apply=%region_19.21 | all-reduce | flops 2 | bytes 16 | tf_op jit(solution)/shard_map/psum | solution.py:52
  372.2 36.1 %psum.137 = f32[]{:T(128)} all-reduce(f32[]{:T(128)} %get-tuple-element.31), channel_id=1, replica_groups=mesh['seg'=8,'sec'=16] {'sec'}, use_global_device_ids=true, to_apply=%region_23.25 | all-reduce | flops 1 | bytes 8 | tf_op jit(solution)/shard_map/psum | solution.py:55
  410.4 4.6 collective-permute-start.9
  418.9 3.0 gather_fusion.4
  421.9 8.1 %multiply_reduce_fusion.4 = (f32[]{:T(128)}, f32[]{:T(128)}, f32[1,8,128,128]{3,2,1,0:T(8,128)S(1)}) fusion(f32[1,8,128,128]{3,2,1,0:T(8,128)S(1)} %get-tuple-element.32, f32[]{:T(128)S(6)} %sqrt.21, bf16[1,8,16,128,128]{4,3,2,1,0:T(8,128)(2,1)} %param.19, bf16[8,16,128,128]{2,3,1,0:T(8,128)(2,1)} %fusion.1, bf16[8,16,128,128]{3,2,1,0:T(8,128)(2,1)} %bitcast.243, ...), kind=kOutput, calls=%fused_computation.92 | convolution fusion | flops 1079377920 | bytes 14155948 | tf_op jit(solution)/shard_map/bkil,bklm->bim/dot_general | solution.py:42
  430.0 38.6 %all-reduce.1 = (f32[]{:T(128)}, f32[]{:T(128)}) all-reduce(f32[]{:T(128)} %get-tuple-element.10, f32[]{:T(128)} %get-tuple-element.9), channel_id=1, replica_groups=mesh['seg'=8,'sec'=16] {'sec'}, use_global_device_ids=true, to_apply=%region_25.27 | all-reduce | flops 2 | bytes 16 | tf_op jit(solution)/shard_map/psum | solution.py:52
  470.7 36.1 %psum.140 = f32[]{:T(128)} all-reduce(f32[]{:T(128)} %get-tuple-element.29), channel_id=1, replica_groups=mesh['seg'=8,'sec'=16] {'sec'}, use_global_device_ids=true, to_apply=%region_29.31 | all-reduce | flops 1 | bytes 8 | tf_op jit(solution)/shard_map/psum | solution.py:55
  508.9 4.8 collective-permute-start.11
  520.4 8.1 %multiply_reduce_fusion.1 = (f32[]{:T(128)}, f32[]{:T(128)}, f32[1,8,128,128]{3,2,1,0:T(8,128)S(1)}) fusion(f32[1,8,128,128]{3,2,1,0:T(8,128)S(1)} %get-tuple-element.30, f32[]{:T(128)S(6)} %sqrt.22, bf16[1,8,16,128,128]{4,3,2,1,0:T(8,128)(2,1)} %param.19, bf16[8,16,128,128]{2,3,1,0:T(8,128)(2,1)} %fusion.1, bf16[8,16,128,128]{3,2,1,0:T(8,128)(2,1)} %bitcast.239, ...), kind=kOutput, calls=%fused_computation.88 | convolution fusion | flops 1079377920 | bytes 14155948 | tf_op jit(solution)/shard_map/bkil,bklm->bim/dot_general | solution.py:42
  528.5 38.6 %all-reduce = (f32[]{:T(128)}, f32[]{:T(128)}) all-reduce(f32[]{:T(128)} %get-tuple-element.8, f32[]{:T(128)} %get-tuple-element.7), channel_id=1, replica_groups=mesh['seg'=8,'sec'=16] {'sec'}, use_global_device_ids=true, to_apply=%region_31.33 | all-reduce | flops 2 | bytes 16 | tf_op jit(solution)/shard_map/psum | solution.py:52
  569.3 36.1 %psum.143 = f32[]{:T(128)} all-reduce(f32[]{:T(128)} %get-tuple-element.27), channel_id=1, replica_groups=mesh['seg'=8,'sec'=16] {'sec'}, use_global_device_ids=true, to_apply=%region_35.37 | all-reduce | flops 1 | bytes 8 | tf_op jit(solution)/shard_map/psum | solution.py:55
  (52 shorter events, 34.8 us)
Async XLA Ops:
  2.1 9.9 %collective-permute-start.1 = (bf16[1,8,128,128]{3,2,1,0:T(8,128)(2,1)S(1)}, bf16[1,8,128,128]{3,2,1,0:T(8,128)(2,1)S(1)}, u32[]{:S(2)}, u32[]{:S(2)}) collective-permute-start(bf16[1,8,128,128]{3,2,1,0:T(8,128)(2,1)S(1)} %get-tuple-element.44), channel_id=1, source_target_pairs={{1,0},{2,1},{3,2},{4,3},{5,4},{6,5},{7,6},{8,7},{9,8},{10,9},{11,1... | collective-permute-start | bytes 786440 | tf_op jit(solution)/shard_map/ppermute | solution.py:17
  3.4 9.8 %collective-permute-start = (bf16[1,8,128,128]{3,2,1,0:T(8,128)(2,1)S(1)}, bf16[1,8,128,128]{3,2,1,0:T(8,128)(2,1)S(1)}, u32[]{:S(2)}, u32[]{:S(2)}) collective-permute-start(bf16[1,8,128,128]{3,2,1,0:T(8,128)(2,1)S(1)} %get-tuple-element.44), channel_id=1, source_target_pairs={{0,1},{1,2},{2,3},{3,4},{4,5},{5,6},{6,7},{7,8},{8,9},{9,10},{10,1... | collective-permute-start | bytes 786440 | tf_op jit(solution)/shard_map/ppermute | solution.py:14
  13.3 3.0 copy-start
  13.3 3.0 copy-start.2
  13.3 3.0 copy-start.4
  105.6 8.3 %collective-permute-start.3 = (bf16[1,8,128,128]{3,2,1,0:T(8,128)(2,1)S(1)}, bf16[1,8,128,128]{3,2,1,0:T(8,128)(2,1)S(1)}, u32[]{:S(2)}, u32[]{:S(2)}) collective-permute-start(bf16[1,8,128,128]{3,2,1,0:T(8,128)(2,1)S(1)} %fusion.263), channel_id=1, source_target_pairs={{1,0},{2,1},{3,2},{4,3},{5,4},{6,5},{7,6},{8,7},{9,8},{10,9},{11,1... | collective-permute-start | bytes 786440 | tf_op jit(solution)/shard_map/ppermute | solution.py:17
  106.9 8.5 %collective-permute-start.2 = (bf16[1,8,128,128]{3,2,1,0:T(8,128)(2,1)S(1)}, bf16[1,8,128,128]{3,2,1,0:T(8,128)(2,1)S(1)}, u32[]{:S(2)}, u32[]{:S(2)}) collective-permute-start(bf16[1,8,128,128]{3,2,1,0:T(8,128)(2,1)S(1)} %fusion.263), channel_id=1, source_target_pairs={{0,1},{1,2},{2,3},{3,4},{4,5},{5,6},{6,7},{7,8},{8,9},{9,10},{10,1... | collective-permute-start | bytes 786440 | tf_op jit(solution)/shard_map/ppermute | solution.py:14
  203.6 11.7 %collective-permute-start.5 = (bf16[1,8,128,128]{3,2,1,0:T(8,128)(2,1)S(1)}, bf16[1,8,128,128]{3,2,1,0:T(8,128)(2,1)S(1)}, u32[]{:S(2)}, u32[]{:S(2)}) collective-permute-start(bf16[1,8,128,128]{3,2,1,0:T(8,128)(2,1)S(1)} %fusion.264), channel_id=1, source_target_pairs={{1,0},{2,1},{3,2},{4,3},{5,4},{6,5},{7,6},{8,7},{9,8},{10,9},{11,1... | collective-permute-start | bytes 786440 | tf_op jit(solution)/shard_map/ppermute | solution.py:17
  204.9 10.5 %collective-permute-start.4 = (bf16[1,8,128,128]{3,2,1,0:T(8,128)(2,1)S(1)}, bf16[1,8,128,128]{3,2,1,0:T(8,128)(2,1)S(1)}, u32[]{:S(2)}, u32[]{:S(2)}) collective-permute-start(bf16[1,8,128,128]{3,2,1,0:T(8,128)(2,1)S(1)} %fusion.264), channel_id=1, source_target_pairs={{0,1},{1,2},{2,3},{3,4},{4,5},{5,6},{6,7},{7,8},{8,9},{9,10},{10,1... | collective-permute-start | bytes 786440 | tf_op jit(solution)/shard_map/ppermute | solution.py:14
  209.5 103.1 %collective-permute-start.8 = (bf16[1,8,128,128]{3,2,1,0:T(8,128)(2,1)S(1)}, bf16[1,8,128,128]{3,2,1,0:T(8,128)(2,1)S(1)}, u32[]{:S(2)}, u32[]{:S(2)}) collective-permute-start(bf16[1,8,128,128]{3,2,1,0:T(8,128)(2,1)S(1)} %get-tuple-element.43), channel_id=1, source_target_pairs={{1,0},{2,1},{3,2},{4,3},{5,4},{6,5},{7,6},{8,7},{9,8},{10,9},{11,1... | collective-permute-start | bytes 786440 | tf_op jit(solution)/shard_map/ppermute | solution.py:17
  210.8 101.8 %collective-permute-start.7 = (bf16[1,8,128,128]{3,2,1,0:T(8,128)(2,1)S(1)}, bf16[1,8,128,128]{3,2,1,0:T(8,128)(2,1)S(1)}, u32[]{:S(2)}, u32[]{:S(2)}) collective-permute-start(bf16[1,8,128,128]{3,2,1,0:T(8,128)(2,1)S(1)} %get-tuple-element.43), channel_id=1, source_target_pairs={{0,1},{1,2},{2,3},{3,4},{4,5},{5,6},{6,7},{7,8},{8,9},{9,10},{10,1... | collective-permute-start | bytes 786440 | tf_op jit(solution)/shard_map/ppermute | solution.py:14
  304.2 11.5 %collective-permute-start.6 = (bf16[1,8,128,128]{3,2,1,0:T(8,128)(2,1)S(1)}, bf16[1,8,128,128]{3,2,1,0:T(8,128)(2,1)S(1)}, u32[]{:S(2)}, u32[]{:S(2)}) collective-permute-start(bf16[1,8,128,128]{3,2,1,0:T(8,128)(2,1)S(1)} %get-tuple-element.33), channel_id=1, source_target_pairs={{0,16},{16,32},{32,48},{48,64},{64,80},{80,96},{96,112},{1,17},{17... | collective-permute-start | bytes 786440 | tf_op jit(solution)/shard_map/ppermute | solution.py:25
  315.7 8.0 %copy-start.1 = (f32[1,8,128,128]{3,2,1,0:T(8,128)S(1)}, f32[1,8,128,128]{3,2,1,0:T(8,128)}, u32[]{:S(2)}) copy-start(f32[1,8,128,128]{3,2,1,0:T(8,128)} %param.15) | copy-start | bytes 1572868
  315.7 8.0 %copy-start.3 = (f32[1,8,128,128]{3,2,1,0:T(8,128)S(1)}, f32[1,8,128,128]{3,2,1,0:T(8,128)}, u32[]{:S(2)}) copy-start(f32[1,8,128,128]{3,2,1,0:T(8,128)} %param.13) | copy-start | bytes 1572868
  409.1 8.3 %collective-permute-start.10 = (bf16[1,8,128,128]{3,2,1,0:T(8,128)(2,1)S(1)}, bf16[1,8,128,128]{3,2,1,0:T(8,128)(2,1)S(1)}, u32[]{:S(2)}, u32[]{:S(2)}) collective-permute-start(bf16[1,8,128,128]{3,2,1,0:T(8,128)(2,1)S(1)} %fusion.265), channel_id=1, source_target_pairs={{1,0},{2,1},{3,2},{4,3},{5,4},{6,5},{7,6},{8,7},{9,8},{10,9},{11,1... | collective-permute-start | bytes 786440 | tf_op jit(solution)/shard_map/ppermute | solution.py:17
  410.4 8.4 %collective-permute-start.9 = (bf16[1,8,128,128]{3,2,1,0:T(8,128)(2,1)S(1)}, bf16[1,8,128,128]{3,2,1,0:T(8,128)(2,1)S(1)}, u32[]{:S(2)}, u32[]{:S(2)}) collective-permute-start(bf16[1,8,128,128]{3,2,1,0:T(8,128)(2,1)S(1)} %fusion.265), channel_id=1, source_target_pairs={{0,1},{1,2},{2,3},{3,4},{4,5},{5,6},{6,7},{7,8},{8,9},{9,10},{10,1... | collective-permute-start | bytes 786440 | tf_op jit(solution)/shard_map/ppermute | solution.py:14
  507.6 8.3 %collective-permute-start.12 = (bf16[1,8,128,128]{3,2,1,0:T(8,128)(2,1)S(1)}, bf16[1,8,128,128]{3,2,1,0:T(8,128)(2,1)S(1)}, u32[]{:S(2)}, u32[]{:S(2)}) collective-permute-start(bf16[1,8,128,128]{3,2,1,0:T(8,128)(2,1)S(1)} %fusion.266), channel_id=1, source_target_pairs={{1,0},{2,1},{3,2},{4,3},{5,4},{6,5},{7,6},{8,7},{9,8},{10,9},{11,1... | collective-permute-start | bytes 786440 | tf_op jit(solution)/shard_map/ppermute | solution.py:17
  508.9 8.5 %collective-permute-start.11 = (bf16[1,8,128,128]{3,2,1,0:T(8,128)(2,1)S(1)}, bf16[1,8,128,128]{3,2,1,0:T(8,128)(2,1)S(1)}, u32[]{:S(2)}, u32[]{:S(2)}) collective-permute-start(bf16[1,8,128,128]{3,2,1,0:T(8,128)(2,1)S(1)} %fusion.266), channel_id=1, source_target_pairs={{0,1},{1,2},{2,3},{3,4},{4,5},{5,6},{6,7},{7,8},{8,9},{9,10},{10,1... | collective-permute-start | bytes 786440 | tf_op jit(solution)/shard_map/ppermute | solution.py:14
where the time goes:
time: 608 us; the launch traced here: 607 us
  blocking collectives  451 us (74%)
  matrix products  55.3 us (9%)
  starting transfers between devices  37.3 us (6%)
  local copies, waits for them, and re-layouts  24.6 us (4%)
  waiting for transfers between devices  15.9 us (3%)
  between operations  13.2 us (2%)
  other arithmetic  9.4 us (2%)
    psum x6, blocking collectives, davidson(): lax.psum((jnp.sum(vector * image), jnp.sum(vector * vector)), 'sec')  235 us
    psum x6, blocking collectives, davidson(): length = lax.psum(jnp.sum(moved * moved), 'sec')  217 us
    dot_general x6, matrix products, operate(): jnp.einsum('bkil,bklm->bim', left_part, right_env[0], preferred_element_t...  47.3 us
    ppermute x6, starting transfers between devices, extended_2(): lax.ppermute(lax.slice_in_dim(block, block.shape[dim] - width, None, axis...  27.6 us
    gather x6, local copies, waits for them, and re-layouts, operate(): picked = jnp.take(extended[0], local_source, axis=0)  18.1 us
  transfers between devices with their start and end apart: 13, of which 8 were waited for; matrix products, arithmetic and copies ran while one was open for 4% of the time, Pallas kernels for 0%

commit v1 on v0

v1 whole, which is shorter than its diff:
```python
import functools

import jax
import jax.numpy as jnp
from jax import lax
from jax.experimental import pallas as pl
from jax.experimental.pallas import tpu as pltpu
from jax.sharding import PartitionSpec as P

STEPS = 3
BLK = 8
TERMS = 16
DIM = 128
QUAD = 4
MESH = pl.DeviceIdType.MESH
F32, BF16 = jnp.float32, jnp.bfloat16


def dot(a, b):
    return jnp.dot(a, b, preferred_element_type=F32)


def folded(x):
    return jnp.sum(x.reshape(DIM // 8, 8, DIM), axis=0)


def kernel(
    nseg, nsec, entries,
    wave0, wave1, onsite0, onsite1, left0, right0, left1, right1, sources, dims,
    out0, out1,
    v, h, hinv, a_own, left, base, right, ext,
    send_v, send_h, send_a, send_hand, send_r,
    land_v, land_h, land_a, land_hand, land_r,
    sums, shift,
    load_sem, out_sem, v_ss, v_rs, h_ss, h_rs, a_ss, a_rs, r_ss, r_rs, hand_ss, hand_rs,
):
    seg, me = lax.axis_index("seg"), lax.axis_index("sec")
    sides = (lax.rem(me + 1, nsec), lax.rem(me + nsec - 1, nsec))
    seg_next, seg_prev = lax.rem(seg + 1, nseg), lax.rem(seg + nseg - 1, nseg)

    def load(i):
        src, dst = (
            (wave0, v.at[0]), (onsite0, h.at[0]), (left0, left), (right0, right.at[0]),
            (wave1, v.at[1]), (onsite1, h.at[1]), (left1, base), (right1, right.at[1]),
        )[i]
        return pltpu.make_async_copy(src, dst, load_sem.at[i])

    def halo(src, land, ss, rs, side):
        return pltpu.make_async_remote_copy(
            src_ref=src, dst_ref=land, send_sem=ss, recv_sem=rs,
            device_id={"sec": sides[side]}, device_id_type=MESH,
        )

    def v_copy(upd, side):
        return halo(send_v.at[upd], land_v.at[upd, side], v_ss.at[upd, side], v_rs.at[upd, side], side)

    def h_copy(upd, side):
        return halo(send_h.at[upd], land_h.at[upd, side], h_ss.at[upd, side], h_rs.at[upd, side], side)

    def a_copy(par, quad, side):
        rows = pl.ds(quad * QUAD, QUAD)
        return halo(send_a.at[rows], land_a.at[par, side, rows], a_ss.at[quad, side], a_rs.at[par, quad, side], side)

    def r_copy(par, d):
        return pltpu.make_async_remote_copy(
            src_ref=send_r, dst_ref=land_r.at[par, d - 1], send_sem=r_ss.at[d - 1], recv_sem=r_rs.at[par, d - 1],
            device_id={"sec": lax.rem(me + d, nsec)}, device_id_type=MESH,
        )

    def hand_copy(quad):
        rows = pl.ds(quad * QUAD, QUAD)
        return pltpu.make_async_remote_copy(
            src_ref=send_hand.at[rows], dst_ref=land_hand.at[rows], send_sem=hand_ss.at[quad], recv_sem=hand_rs.at[quad],
            device_id={"seg": seg_next}, device_id_type=MESH,
        )

    def live(b):
        row = lax.broadcasted_iota(jnp.int32, (DIM, DIM), 0)
        col = lax.broadcasted_iota(jnp.int32, (DIM, DIM), 1)
        limit = dims[b]
        return (row < limit) & (col < limit)

    for i in range(4):
        load(i).start()

    barrier = pltpu.get_barrier_semaphore()
    for d in range(1, nsec):
        pl.semaphore_signal(barrier, inc=1, device_id={"sec": lax.rem(me + d, nsec)}, device_id_type=MESH)
    for other in (seg_next, seg_prev):
        pl.semaphore_signal(barrier, inc=1, device_id={"seg": other}, device_id_type=MESH)
    pl.semaphore_wait(barrier, nsec + 1)

    def start_wave(upd):
        def one(b, _):
            w = jnp.where(live(b), v[upd, b], 0.0)
            v[upd, b] = w
            send_v[upd, b] = w.astype(BF16)
            return 0

        lax.fori_loop(0, BLK, one, 0, unroll=2)

    def start_onsite(upd):
        def one(b, _):
            inverse = 1.0 / (h[upd, b] + 1.0)
            hinv[upd, b] = inverse
            send_h[upd, b] = inverse.astype(BF16)
            return 0

        lax.fori_loop(0, BLK, one, 0, unroll=2)

    load(0).wait()
    start_wave(0)
    for side in range(2):
        v_copy(0, side).start()
    load(1).wait()
    start_onsite(0)
    for side in range(2):
        h_copy(0, side).start()
    for i in range(4, 8):
        load(i).start()
    load(4).wait()
    start_wave(1)
    load(5).wait()
    start_onsite(1)
    shift[...] = jnp.ones_like(shift)
    load(2).wait()
    load(3).wait()

    def build():
        def quad_step(quad, _):
            hand_copy(quad).wait_recv()

            def one(i, _):
                b = quad * QUAD + i
                handed = jnp.where(seg > 0, land_hand[b], jnp.zeros((DIM, DIM), BF16))
                turned = handed.T
                carried = dot(base[b].reshape(TERMS * DIM, DIM), handed).astype(BF16)
                for k in range(0, TERMS, 2):
                    pair = jnp.concatenate([carried[k * DIM : (k + 1) * DIM], carried[(k + 1) * DIM : (k + 2) * DIM]], axis=1)
                    added = dot(turned, pair)
                    for q in range(2):
                        term = added[:, q * DIM : (q + 1) * DIM] * (1.0 / DIM)
                        left[b, k + q] = (base[b, k + q].astype(F32) + term).astype(BF16)
                return 0

            lax.fori_loop(0, QUAD, one, 0, unroll=2)
            return 0

        lax.fori_loop(0, BLK // QUAD, quad_step, 0)

    def begin(upd):
        for side in range(2):
            v_copy(upd, side).wait_recv()

        def one(b, _):
            ext[b] = land_v[upd, 0, b]
            ext[BLK + b] = send_v[upd, b]
            ext[2 * BLK + b] = land_v[upd, 1, b]
            return 0

        lax.fori_loop(0, BLK, one, 0, unroll=2)

    def step(n, _):
        upd, it = n // STEPS, lax.rem(n, STEPS)
        par = lax.rem(n, 2)

        @pl.when(it == 0)
        def _():
            begin(upd)

        @pl.when(n == STEPS)
        def _():
            load(6).wait()
            load(7).wait()
            build()
            for quad in range(BLK // QUAD):
                hand_copy(quad).wait_send()

        sums[...] = jnp.zeros_like(sums)
        first = (me - 1) * BLK
        guess = shift[0:1, 0:1]

        def quad_step(quad, _):
            for i in range(QUAD):
                b = quad * QUAD + i
                parts = [
                    dot(left[b, k], ext[jnp.clip(sources[b, k] - first, 0, 3 * BLK - 1)]).astype(BF16)
                    for k in range(TERMS)
                ]
                terms = dot(jnp.concatenate(parts, axis=1), right[upd, b].reshape(TERMS * DIM, DIM))
                vec, inverse = v[upd, b], hinv[upd, b]
                image = h[upd, b] * vec + jnp.where(live(b), terms, 0.0)
                along = vec * inverse
                part = vec - (image - guess * vec) * inverse
                a_own[b] = part
                send_a[b] = part.astype(BF16)
                sums[0] += folded(vec * image)
                sums[1] += folded(vec * vec)
                sums[2] += folded(part * part)
                sums[3] += folded(part * along)
                sums[4] += folded(along * along)

            @pl.when(it < STEPS - 1)
            def _():
                for side in range(2):
                    a_copy(par, quad, side).start()

            return 0

        lax.fori_loop(0, BLK // QUAD, quad_step, 0)

        row = lax.broadcasted_iota(jnp.int32, (8, DIM), 0)
        packet = jnp.zeros((8, DIM), F32)
        for i in range(5):
            packet = jnp.where(row == i, jnp.sum(sums[i], axis=0, keepdims=True), packet)
        send_r[...] = packet
        for d in range(1, nsec):
            r_copy(par, d).start()

        @pl.when(n == 0)
        def _():
            for side in range(2):
                v_copy(1, side).start()

        @pl.when(n == 1)
        def _():
            for side in range(2):
                h_copy(1, side).start()

        for d in range(1, nsec):
            r_copy(par, d).wait_recv()
        total = packet
        for d in range(1, nsec):
            total = total + land_r[par, d - 1]
        total = jnp.sum(total, axis=1, keepdims=True)
        quotient = total[0:1] / total[1:2]
        delta = quotient - guess
        square = jnp.maximum(total[2:3] + 2.0 * delta * total[3:4] + delta * delta * total[4:5], 0.0)
        scale = 1.0 / jnp.sqrt(square / entries + 1e-06)
        shift[...] = jnp.broadcast_to(quotient, shift.shape)

        def own(b, _):
            vec = scale * (a_own[b] + delta * (v[upd, b] * hinv[upd, b]))
            v[upd, b] = vec
            ext[BLK + b] = vec.astype(BF16)
            send_hand[b] = vec.astype(BF16)
            return 0

        lax.fori_loop(0, BLK, own, 0, unroll=2)

        @pl.when(it < STEPS - 1)
        def _():
            @pl.when(it == 0)
            def _():
                for side in range(2):
                    h_copy(upd, side).wait_recv()

            for quad in range(BLK // QUAD):
                for side in range(2):
                    a_copy(par, quad, side).wait_recv()

            def near(b, _):
                for side in range(2):
                    at = 2 * BLK * side + b
                    along = ext[at].astype(F32) * land_h[upd, side, b].astype(F32)
                    ext[at] = (scale * (land_a[par, side, b].astype(F32) + delta * along)).astype(BF16)
                return 0

            lax.fori_loop(0, BLK, near, 0)
            for quad in range(BLK // QUAD):
                for side in range(2):
                    a_copy(par, quad, side).wait_send()

        @pl.when(n == STEPS - 1)
        def _():
            for quad in range(BLK // QUAD):
                hand_copy(quad).start()
            pltpu.make_async_copy(v.at[0], out0, out_sem.at[0]).start()
            shift[...] = jnp.ones_like(shift)

        for d in range(1, nsec):
            r_copy(par, d).wait_send()
        return 0

    lax.fori_loop(0, 2 * STEPS, step, 0)
    last = pltpu.make_async_copy(v.at[1], out1, out_sem.at[1])
    last.start()
    for upd in range(2):
        for side in range(2):
            v_copy(upd, side).wait_send()
            h_copy(upd, side).wait_send()
    pltpu.make_async_copy(v.at[0], out0, out_sem.at[0]).wait()
    last.wait()


def on_device(nseg, nsec, *args):
    entries = float(nsec * BLK * DIM * DIM)
    anywhere = pl.BlockSpec(memory_space=pl.ANY)
    scalars = pl.BlockSpec(memory_space=pltpu.SMEM)
    waves, envs = (BLK, DIM, DIM), (BLK, TERMS, DIM, DIM)
    dma = pltpu.SemaphoreType.DMA
    big = [a[0] for a in args[:8]]
    outs = pl.pallas_call(
        functools.partial(kernel, nseg, nsec, entries),
        out_shape=[jax.ShapeDtypeStruct(waves, F32)] * 2,
        in_specs=[anywhere] * 8 + [scalars] * 2,
        out_specs=[anywhere] * 2,
        scratch_shapes=[
            pltpu.VMEM((2, *waves), F32),
            pltpu.VMEM((2, *waves), F32),
            pltpu.VMEM((2, *waves), F32),
            pltpu.VMEM(waves, F32),
            pltpu.VMEM(envs, BF16),
            pltpu.VMEM(envs, BF16),
            pltpu.VMEM((2, *envs), BF16),
            pltpu.VMEM((3 * BLK, DIM, DIM), BF16),
            pltpu.VMEM((2, *waves), BF16),
            pltpu.VMEM((2, *waves), BF16),
            pltpu.VMEM(waves, BF16),
            pltpu.VMEM(waves, BF16),
            pltpu.VMEM((8, DIM), F32),
            pltpu.VMEM((2, 2, *waves), BF16),
            pltpu.VMEM((2, 2, *waves), BF16),
            pltpu.VMEM((2, 2, *waves), BF16),
            pltpu.VMEM(waves, BF16),
            pltpu.VMEM((2, nsec - 1, 8, DIM), F32),
            pltpu.VMEM((5, 8, DIM), F32),
            pltpu.VMEM((8, DIM), F32),
            dma((8,)),
            dma((2,)),
            dma((2, 2)),
            dma((2, 2)),
            dma((2, 2)),
            dma((2, 2)),
            dma((BLK // QUAD, 2)),
            dma((2, BLK // QUAD, 2)),
            dma((nsec - 1,)),
            dma((2, nsec - 1)),
            dma((BLK // QUAD,)),
            dma((BLK // QUAD,)),
        ],
        compiler_params=pltpu.CompilerParams(
            collective_id=0, has_side_effects=True, vmem_limit_bytes=52 * 2**20
        ),
        cost_estimate=pl.CostEstimate(
            flops=7 * BLK * TERMS * 4 * DIM**3, bytes_accessed=20 * 2**20, transcendentals=0
        ),
        name="updates",
    )(*big, *args[8:])
    return tuple(o[None] for o in outs)


def solution(mesh):
    wave, env = P("seg", "sec", None, None), P("seg", "sec", None, None, None)
    return jax.shard_map(
        functools.partial(on_device, mesh.shape["seg"], mesh.shape["sec"]),
        mesh=mesh,
        in_specs=(wave, wave, wave, wave, env, env, env, env, P("sec", None), P("sec")),
        out_specs=(wave, wave),
        check_vma=False,
    )
```

time: 608 us -> 91.7 us (0.15)
  blocking collectives: 451 us -> 0 us
  Pallas kernels: 0 us -> 86.9 us
  matrix products: 55.3 us -> 0 us
  starting transfers between devices: 37.3 us -> 0 us
  local copies, waits for them, and re-layouts: 24.6 us -> 3.96 us
  waiting for transfers between devices: 15.9 us -> 0 us
  between operations: 13.2 us -> 0.65 us
  other arithmetic: 9.4 us -> 0 us
    psum x12 -> x0, blocking collectives: 451 us -> none  [the longest x6 235 us: davidson(): lax.psum((jnp.sum(vector * image), jnp.sum(vector * vector)), 'sec')]
    pallas_call x0 -> x1, Pallas kernels: none -> 86.9 us  [on_device(): pl.pallas_call(functools.partial(kernel, nseg, nsec, entries), out_shape=...]
    dot_general x7 -> x0, matrix products: 55.3 us -> none  [the longest x6 47.3 us: operate(): jnp.einsum('bkil,bklm->bim', left_part, right_env[0], preferred_element_t...]
    ppermute x13 -> x0, starting transfers between devices: 37.3 us -> none  [the longest x6 27.6 us: extended_2(): lax.ppermute(lax.slice_in_dim(block, block.shape[dim] - width, None, axis...]
    gather x6 -> x0, local copies, waits for them, and re-layouts: 18.1 us -> none  [operate(): picked = jnp.take(extended[0], local_source, axis=0)]
    ppermute x13 -> x0, waiting for transfers between devices: 15.9 us -> none  [the longest x6 10.3 us: extended_2(): lax.ppermute(lax.slice_in_dim(block, 0, width, axis=dim), axis, backward)]
  transfers between devices with their start and end apart: 13 -> 0, of which waited for: 8 -> 0; matrix products, arithmetic and copies ran while one was open for 4% -> 0% of each run, Pallas kernels for 0% -> 0%
where the time goes in v1:
time: 91.7 us; the launch traced here: 91.5 us
  Pallas kernels  86.9 us (95%)
  local copies, waits for them, and re-layouts  3.96 us (4%)
    pallas_call x1, Pallas kernels, on_device(): pl.pallas_call(functools.partial(kernel, nseg, nsec, entries), out_shape=...  86.9 us
    unnamed x8, local copies, waits for them, and re-layouts  3.96 us

profile of v1, /device:TPU:32, one launch (start us, length us, event | category | flops | bytes accessed | tf_op | source)
XLA Modules:
  0.0 91.5 jit_solution(10851658439923067993)
XLA Ops:
  0.6 0.0 copy-start
  0.6 1.0 %copy-done = f32[1,8,128,128]{3,2,1,0:T(8,128)S(1)} copy-done((f32[1,8,128,128]{3,2,1,0:T(8,128)S(1)}, f32[1,8,128,128]{3,2,1,0:T(8,128)}, u32[]{:S(2)}) %copy-start) | copy-done | bytes 524312
  1.7 0.0 copy-start.1
  1.7 0.7 copy-done.1
  2.4 0.0 copy-start.2
  2.4 0.7 copy-done.2
  3.0 86.9 %updates.1 = (f32[8,128,128]{2,1,0:T(8,128)S(1)}, f32[8,128,128]{2,1,0:T(8,128)S(1)}) custom-call(f32[8,128,128]{2,1,0:T(8,128)S(1)} %bitcast.12, f32[8,128,128]{2,1,0:T(8,128)} %bitcast.17, f32[8,128,128]{2,1,0:T(8,128)} %bitcast.18, f32[8,128,128]{2,1,0:T(8,128)} %bitcast.19, bf16[8,16,128,128]{3,2,1,0:T(8,128)(2,1)} %bitcast.13, ...), custom_call_target="tpu_custom_call" | custom-call | flops 7516192768 | bytes 20971520 | tf_op jit(solution)/shard_map/updates/pallas_call | solution.py:303
  89.9 0.8 copy.14
  90.7 0.8 copy.15
Async XLA Ops:
  0.6 1.0 %copy-start = (f32[1,8,128,128]{3,2,1,0:T(8,128)S(1)}, f32[1,8,128,128]{3,2,1,0:T(8,128)}, u32[]{:S(2)}) copy-start(f32[1,8,128,128]{3,2,1,0:T(8,128)} %param.10) | copy-start | bytes 1572868
  1.7 0.7 copy-start.1
  2.4 0.7 copy-start.2

commit v2 on v1

v2 whole, which is shorter than its diff:
```python
import functools

import jax
import jax.numpy as jnp
from jax import lax
from jax.experimental import pallas as pl
from jax.experimental.pallas import tpu as pltpu
from jax.sharding import PartitionSpec as P

STEPS = 3
BLK = 8
TERMS = 16
DIM = 128
QUAD = 4
PAIR = 2
MESH = pl.DeviceIdType.MESH
F32, BF16 = jnp.float32, jnp.bfloat16


def dot(a, b):
    return jnp.dot(a, b, preferred_element_type=F32)


def folded(x):
    return jnp.sum(x.reshape(DIM // 8, 8, DIM), axis=0)


def kernel(
    nseg, nsec, entries,
    wave0, wave1, onsite0, onsite1, left0, right0, left1, right1, sources_in, dims_in,
    out0, out1,
    v, h, hinv, a_own, left, base, right, ext,
    send_v, send_h, send_a, send_b, send_scale, send_r,
    land_v, land_h, land_a, land_hand_a, land_hand_b, land_scale, land_r, near_b,
    sums, shift, sources, dims,
    load_sem, out_sem, v_ss, v_rs, h_ss, h_rs, a_ss, a_rs, r_ss, r_rs, hand_ss, hand_rs,
):
    seg, me = lax.axis_index("seg"), lax.axis_index("sec")
    sides = (lax.rem(me + 1, nsec), lax.rem(me + nsec - 1, nsec))
    seg_next, seg_prev = lax.rem(seg + 1, nseg), lax.rem(seg + nseg - 1, nseg)

    def load(i):
        src, dst = (
            (wave0, v.at[0]), (onsite0, h.at[0]), (left0, left), (right0, right.at[0]),
            (wave1, v.at[1]), (onsite1, h.at[1]), (left1, base), (right1, right.at[1]),
            (dims_in, dims), (sources_in, sources),
        )[i]
        return pltpu.make_async_copy(src, dst, load_sem.at[i])

    def halo(src, land, ss, rs, side):
        return pltpu.make_async_remote_copy(
            src_ref=src, dst_ref=land, send_sem=ss, recv_sem=rs,
            device_id={"sec": sides[side]}, device_id_type=MESH,
        )

    def v_copy(upd, side):
        return halo(send_v.at[upd], land_v.at[upd, side], v_ss.at[upd, side], v_rs.at[upd, side], side)

    def h_copy(upd, side):
        return halo(send_h.at[upd], land_h.at[upd, side], h_ss.at[upd, side], h_rs.at[upd, side], side)

    def a_copy(par, pair, side):
        rows = pl.ds(pair * PAIR, PAIR)
        return halo(send_a.at[rows], land_a.at[par, side, rows], a_ss.at[pair, side], a_rs.at[par, pair, side], side)

    ny = 4 if nsec % 4 == 0 and nsec > 4 else 2
    nx = nsec // ny
    away = sorted(
        ((dx, dy) for dx in range(nx) for dy in range(ny) if (dx, dy) != (0, 0)),
        key=lambda p: -(min(p[0], nx - p[0]) + min(p[1], ny - p[1])),
    )

    def peer(dx, dy):
        return lax.rem(me // ny + dx, nx) * ny + lax.rem(lax.rem(me, ny) + dy, ny)

    def r_copy(par, i):
        return pltpu.make_async_remote_copy(
            src_ref=send_r, dst_ref=land_r.at[par, i], send_sem=r_ss, recv_sem=r_rs.at[par],
            device_id={"sec": peer(*away[i])}, device_id_type=MESH,
        )

    def r_all(par, sem):
        return pltpu.make_async_copy(land_r.at[par], land_r.at[par], sem)

    def hand_copy(i):
        src, dst = ((send_b, land_hand_b), (send_a, land_hand_a), (send_scale, land_scale))[i]
        return pltpu.make_async_remote_copy(
            src_ref=src, dst_ref=dst, send_sem=hand_ss.at[i], recv_sem=hand_rs.at[i],
            device_id={"seg": seg_next}, device_id_type=MESH,
        )

    def live(b):
        row = lax.broadcasted_iota(jnp.int32, (DIM, DIM), 0)
        col = lax.broadcasted_iota(jnp.int32, (DIM, DIM), 1)
        limit = dims[b]
        return (row < limit) & (col < limit)

    for i in (0, 8, 1, 9, 2, 3):
        load(i).start()

    barrier = pltpu.get_barrier_semaphore()
    for d in range(1, nsec):
        pl.semaphore_signal(barrier, inc=1, device_id={"sec": lax.rem(me + d, nsec)}, device_id_type=MESH)
    for other in (seg_next, seg_prev):
        pl.semaphore_signal(barrier, inc=1, device_id={"seg": other}, device_id_type=MESH)
    pl.semaphore_wait(barrier, nsec + 1)

    def start_wave(upd):
        def one(b, _):
            w = jnp.where(live(b), v[upd, b], 0.0)
            v[upd, b] = w
            send_v[upd, b] = w.astype(BF16)
            return 0

        lax.fori_loop(0, BLK, one, 0, unroll=2)

    def start_onsite(upd):
        def one(b, _):
            inverse = 1.0 / (h[upd, b] + 1.0)
            hinv[upd, b] = inverse
            send_h[upd, b] = inverse.astype(BF16)
            return 0

        lax.fori_loop(0, BLK, one, 0, unroll=2)

    load(0).wait()
    load(8).wait()
    start_wave(0)
    for side in range(2):
        v_copy(0, side).start()
    load(1).wait()
    start_onsite(0)
    for i in range(4, 8):
        load(i).start()
    load(4).wait()
    start_wave(1)
    load(5).wait()
    start_onsite(1)
    for side in range(2):
        v_copy(0, side).wait_send()
    for side in range(2):
        h_copy(0, side).start()
    for i in (9, 2, 3):
        load(i).wait()

    def build():
        for i in range(3):
            hand_copy(i).wait_recv()
        scale, delta = land_scale[0:1, 0:1], land_scale[1:2, 0:1]

        def one(b, _):
            moved = scale * (land_hand_a[b].astype(F32) + delta * land_hand_b[b].astype(F32))
            handed = jnp.where(seg > 0, moved, 0.0).astype(BF16)
            turned = handed.T
            carried = dot(base[b].reshape(TERMS * DIM, DIM), handed).astype(BF16)
            for k in range(0, TERMS, 2):
                pair = jnp.concatenate([carried[k * DIM : (k + 1) * DIM], carried[(k + 1) * DIM : (k + 2) * DIM]], axis=1)
                added = dot(turned, pair)
                for q in range(2):
                    term = added[:, q * DIM : (q + 1) * DIM] * (1.0 / DIM)
                    left[b, k + q] = (base[b, k + q].astype(F32) + term).astype(BF16)
            return 0

        lax.fori_loop(0, BLK, one, 0, unroll=4)

    def begin(upd):
        for side in range(2):
            v_copy(upd, side).wait_recv()

        def one(b, _):
            ext[b] = land_v[upd, 0, b]
            ext[BLK + b] = send_v[upd, b]
            ext[2 * BLK + b] = land_v[upd, 1, b]
            return 0

        lax.fori_loop(0, BLK, one, 0, unroll=2)
        shift[...] = jnp.ones_like(shift)

    def step(upd, it, more):
        par = lax.rem(upd * STEPS + it, 2)
        sums[...] = jnp.zeros_like(sums)
        first = (me - 1) * BLK
        guess = shift[0:1, 0:1]

        def quad_step(quad, _):
            for i in range(QUAD):
                b = quad * QUAD + i
                parts = [
                    dot(left[b, k], ext[jnp.clip(sources[b, k] - first, 0, 3 * BLK - 1)]).astype(BF16)
                    for k in range(TERMS)
                ]
                terms = dot(jnp.concatenate(parts, axis=1), right[upd, b].reshape(TERMS * DIM, DIM))
                vec, inverse = v[upd, b], hinv[upd, b]
                image = h[upd, b] * vec + jnp.where(live(b), terms, 0.0)
                along = vec * inverse
                part = vec - (image - guess * vec) * inverse
                a_own[b] = part
                send_a[b] = part.astype(BF16)
                sums[0] += folded(vec * image)
                sums[1] += folded(vec * vec)
                sums[2] += folded(part * part)
                sums[3] += folded(part * along)
                sums[4] += folded(along * along)
                if more and i % PAIR == PAIR - 1:
                    for side in range(2):
                        a_copy(it, quad * (QUAD // PAIR) + i // PAIR, side).start()
            return 0

        lax.fori_loop(0, BLK // QUAD, quad_step, 0)

        row = lax.broadcasted_iota(jnp.int32, (8, DIM), 0)
        packet = jnp.zeros((8, DIM), F32)
        for i in range(5):
            packet = jnp.where(row == i, jnp.sum(sums[i], axis=0, keepdims=True), packet)
        send_r[...] = packet
        for i in range(nsec - 1):
            r_copy(par, i).start()

        if more:

            @pl.when(it == 0)
            def _():
                for side in range(2):
                    h_copy(upd, side).wait_recv()

            def toward(b, _):
                for side in range(2):
                    near_b[side, b] = ext[2 * BLK * side + b].astype(F32) * land_h[upd, side, b].astype(F32)
                return 0

            lax.fori_loop(0, BLK, toward, 0)
        else:

            @pl.when(upd == 0)
            def _():
                hand_copy(1).start()

        r_all(par, r_rs.at[par]).wait()
        total = packet + jnp.sum(land_r[par], axis=0)
        total = jnp.sum(total, axis=1, keepdims=True)
        quotient = total[0:1] / total[1:2]
        delta = quotient - guess
        square = jnp.maximum(total[2:3] + 2.0 * delta * total[3:4] + delta * delta * total[4:5], 0.0)
        scale = 1.0 / jnp.sqrt(square / entries + 1e-06)
        shift[...] = jnp.broadcast_to(quotient, shift.shape)

        if not more:

            @pl.when(upd == 0)
            def _():
                send_scale[...] = jnp.where(row == 0, scale, delta)
                hand_copy(2).start()
                for side in range(2):
                    h_copy(1, side).start()

        def own(b, _):
            vec = scale * (a_own[b] + delta * (v[upd, b] * hinv[upd, b]))
            v[upd, b] = vec
            if more:
                ext[BLK + b] = vec.astype(BF16)
            return 0

        lax.fori_loop(0, BLK, own, 0, unroll=2)

        if more:
            for pair in range(BLK // PAIR):
                for side in range(2):
                    a_copy(it, pair, side).wait_recv()

            def near(b, _):
                for side in range(2):
                    ext[2 * BLK * side + b] = (
                        scale * (land_a[it, side, b].astype(F32) + delta * near_b[side, b])
                    ).astype(BF16)
                return 0

            lax.fori_loop(0, BLK, near, 0, unroll=2)
            for pair in range(BLK // PAIR):
                for side in range(2):
                    a_copy(it, pair, side).wait_send()
        r_all(par, r_ss).wait()

    def update(upd, _):
        begin(upd)

        @pl.when(upd == 1)
        def _():
            load(6).wait()
            load(7).wait()
            build()
            for i in range(3):
                hand_copy(i).wait_send()

        def each(it, _):
            step(upd, it, True)
            return 0

        lax.fori_loop(0, STEPS - 1, each, 0)

        @pl.when(upd == 0)
        def _():
            for side in range(2):
                v_copy(1, side).start()

            def one(b, _):
                send_b[b] = (v[0, b] * hinv[0, b]).astype(BF16)
                return 0

            lax.fori_loop(0, BLK, one, 0)
            hand_copy(0).start()

        step(upd, STEPS - 1, False)

        @pl.when(upd == 0)
        def _():
            pltpu.make_async_copy(v.at[0], out0, out_sem.at[0]).start()

        return 0

    lax.fori_loop(0, 2, update, 0)
    last = pltpu.make_async_copy(v.at[1], out1, out_sem.at[1])
    last.start()
    for side in range(2):
        h_copy(0, side).wait_send()
        v_copy(1, side).wait_send()
        h_copy(1, side).wait_send()
    pltpu.make_async_copy(v.at[0], out0, out_sem.at[0]).wait()
    last.wait()


def on_device(nseg, nsec, *args):
    entries = float(nsec * BLK * DIM * DIM)
    hbm = pl.BlockSpec(memory_space=pltpu.HBM)
    waves, envs = (BLK, DIM, DIM), (BLK, TERMS, DIM, DIM)
    dma = pltpu.SemaphoreType.DMA
    big = [a[0] for a in args[:8]]
    outs = pl.pallas_call(
        functools.partial(kernel, nseg, nsec, entries),
        out_shape=[jax.ShapeDtypeStruct(waves, F32)] * 2,
        in_specs=[hbm] * 10,
        out_specs=[pl.BlockSpec(memory_space=pl.ANY)] * 2,
        scratch_shapes=[
            pltpu.VMEM((2, *waves), F32),
            pltpu.VMEM((2, *waves), F32),
            pltpu.VMEM((2, *waves), F32),
            pltpu.VMEM(waves, F32),
            pltpu.VMEM(envs, BF16),
            pltpu.VMEM(envs, BF16),
            pltpu.VMEM((2, *envs), BF16),
            pltpu.VMEM((3 * BLK, DIM, DIM), BF16),
            pltpu.VMEM((2, *waves), BF16),
            pltpu.VMEM((2, *waves), BF16),
            pltpu.VMEM(waves, BF16),
            pltpu.VMEM(waves, BF16),
            pltpu.VMEM((8, DIM), F32),
            pltpu.VMEM((8, DIM), F32),
            pltpu.VMEM((2, 2, *waves), BF16),
            pltpu.VMEM((2, 2, *waves), BF16),
            pltpu.VMEM((2, 2, *waves), BF16),
            pltpu.VMEM(waves, BF16),
            pltpu.VMEM(waves, BF16),
            pltpu.VMEM((8, DIM), F32),
            pltpu.VMEM((2, nsec - 1, 8, DIM), F32),
            pltpu.VMEM((2, *waves), F32),
            pltpu.VMEM((5, 8, DIM), F32),
            pltpu.VMEM((8, DIM), F32),
            pltpu.SMEM((BLK, TERMS), jnp.int32),
            pltpu.SMEM((BLK,), jnp.int32),
            dma((10,)),
            dma((2,)),
            dma((2, 2)),
            dma((2, 2)),
            dma((2, 2)),
            dma((2, 2)),
            dma((BLK // PAIR, 2)),
            dma((2, BLK // PAIR, 2)),
            dma,
            dma((2,)),
            dma((3,)),
            dma((3,)),
        ],
        compiler_params=pltpu.CompilerParams(
            collective_id=0, has_side_effects=True, vmem_limit_bytes=60 * 2**20
        ),
        cost_estimate=pl.CostEstimate(
            flops=7 * BLK * TERMS * 4 * DIM**3, bytes_accessed=20 * 2**20, transcendentals=0
        ),
        name="updates",
    )(*big, *args[8:])
    return tuple(o[None] for o in outs)


def solution(mesh):
    wave, env = P("seg", "sec", None, None), P("seg", "sec", None, None, None)
    return jax.shard_map(
        functools.partial(on_device, mesh.shape["seg"], mesh.shape["sec"]),
        mesh=mesh,
        in_specs=(wave, wave, wave, wave, env, env, env, env, P("sec", None), P("sec")),
        out_specs=(wave, wave),
        check_vma=False,
    )
```

time: 91.7 us -> 84.4 us (0.920)
  Pallas kernels: 86.9 us -> 79.8 us
    pallas_call x1, Pallas kernels: 86.9 us -> 79.8 us  [on_device(): pl.pallas_call(functools.partial(kernel, nseg, nsec, entries), out_shape=...]
    unnamed x8 -> x2, local copies, waits for them, and re-layouts: 3.96 us -> 3.74 us
where the time goes in v2:
time: 84.4 us; the launch traced here: 84.2 us
  Pallas kernels  79.8 us (95%)
  local copies, waits for them, and re-layouts  3.74 us (4%)
    pallas_call x1, Pallas kernels, on_device(): pl.pallas_call(functools.partial(kernel, nseg, nsec, entries), out_shape=...  79.8 us
    unnamed x2, local copies, waits for them, and re-layouts  3.74 us

profile of v2, /device:TPU:32, one launch (start us, length us, event | category | flops | bytes accessed | tf_op | source)
XLA Modules:
  0.0 84.2 jit_solution(3694107451312352695)
XLA Ops:
  0.6 79.8 %updates.1 = (f32[8,128,128]{2,1,0:T(8,128)}, f32[8,128,128]{2,1,0:T(8,128)}) custom-call(f32[8,128,128]{2,1,0:T(8,128)} %bitcast.16, f32[8,128,128]{2,1,0:T(8,128)} %bitcast.17, f32[8,128,128]{2,1,0:T(8,128)} %bitcast.18, f32[8,128,128]{2,1,0:T(8,128)} %bitcast.19, bf16[8,16,128,128]{3,2,1,0:T(8,128)(2,1)} %bitcast.12, bf16[8,16,128,128]{3,2,1,0:T(8,128)(2,1)} %bitcast.13, ...), custom_call_target="tpu_custom_call" | custom-call | flops 7516192768 | bytes 20971520 | tf_op jit(solution)/shard_map/updates/pallas_call | solution.py:337
  80.5 1.9 %copy.14 = f32[1,8,128,128]{3,2,1,0:T(8,128)} copy(f32[1,8,128,128]{3,2,1,0:T(8,128)} %bitcast.11) | data formatting | bytes 1048576
  82.4 1.9 %copy.15 = f32[1,8,128,128]{3,2,1,0:T(8,128)} copy(f32[1,8,128,128]{3,2,1,0:T(8,128)} %bitcast.10) | data formatting | bytes 1048576

commit v3 on v2

--- a/solution.py
+++ b/solution.py
@@ -61,7 +61,10 @@
 
     def a_copy(par, pair, side):
         rows = pl.ds(pair * PAIR, PAIR)
-        return halo(send_a.at[rows], land_a.at[par, side, rows], a_ss.at[pair, side], a_rs.at[par, pair, side], side)
+        return halo(send_a.at[rows], land_a.at[par, side, rows], a_ss, a_rs.at[par], side)
+
+    def a_all(par, sem):
+        return pltpu.make_async_copy(land_a.at[par], land_a.at[par], sem)
 
     ny = 4 if nsec % 4 == 0 and nsec > 4 else 2
     nx = nsec // ny
@@ -70,13 +73,12 @@
         key=lambda p: -(min(p[0], nx - p[0]) + min(p[1], ny - p[1])),
     )
 
-    def peer(dx, dy):
-        return lax.rem(me // ny + dx, nx) * ny + lax.rem(lax.rem(me, ny) + dy, ny)
+    peers = [lax.rem(me // ny + dx, nx) * ny + lax.rem(lax.rem(me, ny) + dy, ny) for dx, dy in away]
 
     def r_copy(par, i):
         return pltpu.make_async_remote_copy(
             src_ref=send_r, dst_ref=land_r.at[par, i], send_sem=r_ss, recv_sem=r_rs.at[par],
-            device_id={"sec": peer(*away[i])}, device_id_type=MESH,
+            device_id={"sec": peers[i]}, device_id_type=MESH,
         )
 
     def r_all(par, sem):
@@ -88,6 +90,10 @@
             src_ref=src, dst_ref=dst, send_sem=hand_ss.at[i], recv_sem=hand_rs.at[i],
             device_id={"seg": seg_next}, device_id_type=MESH,
         )
+
+    def result(upd, part):
+        rows = pl.ds(part * QUAD, QUAD)
+        return pltpu.make_async_copy(v.at[upd, rows], (out0, out1)[upd].at[rows], out_sem.at[upd, part])
 
     def live(b):
         row = lax.broadcasted_iota(jnp.int32, (DIM, DIM), 0)
@@ -201,9 +207,16 @@
                 sums[2] += folded(part * part)
                 sums[3] += folded(part * along)
                 sums[4] += folded(along * along)
-                if more and i % PAIR == PAIR - 1:
+                if more and i % PAIR == PAIR - 1 and i < QUAD - 1:
                     for side in range(2):
                         a_copy(it, quad * (QUAD // PAIR) + i // PAIR, side).start()
+            if more:
+
+                @pl.when(quad == 0)
+                def _():
+                    for side in range(2):
+                        a_copy(it, QUAD // PAIR - 1, side).start()
+
             return 0
 
         lax.fori_loop(0, BLK // QUAD, quad_step, 0)
@@ -217,6 +230,8 @@
             r_copy(par, i).start()
 
         if more:
+            for side in range(2):
+                a_copy(it, BLK // PAIR - 1, side).start()
 
             @pl.when(it == 0)
             def _():
@@ -260,12 +275,23 @@
                 ext[BLK + b] = vec.astype(BF16)
             return 0
 
-        lax.fori_loop(0, BLK, own, 0, unroll=2)
-
         if more:
-            for pair in range(BLK // PAIR):
-                for side in range(2):
-                    a_copy(it, pair, side).wait_recv()
+            lax.fori_loop(0, BLK, own, 0, unroll=4)
+        else:
+            for part in range(2):
+                lax.fori_loop(part * QUAD, (part + 1) * QUAD, own, 0, unroll=4)
+
+                @pl.when(upd == 0)
+                def _():
+                    result(0, part).start()
+
+                @pl.when(upd == 1)
+                def _():
+                    result(1, part).start()
+
+
+        if more:
+            a_all(it, a_rs.at[it]).wait()
 
             def near(b, _):
                 for side in range(2):
@@ -275,9 +301,7 @@
                 return 0
 
             lax.fori_loop(0, BLK, near, 0, unroll=2)
-            for pair in range(BLK // PAIR):
-                for side in range(2):
-                    a_copy(it, pair, side).wait_send()
+            a_all(it, a_ss).wait()
         r_all(par, r_ss).wait()
 
     def update(upd, _):
@@ -311,26 +335,33 @@
 
         step(upd, STEPS - 1, False)
 
-        @pl.when(upd == 0)
-        def _():
-            pltpu.make_async_copy(v.at[0], out0, out_sem.at[0]).start()
-
         return 0
 
     lax.fori_loop(0, 2, update, 0)
-    last = pltpu.make_async_copy(v.at[1], out1, out_sem.at[1])
-    last.start()
     for side in range(2):
         h_copy(0, side).wait_send()
         v_copy(1, side).wait_send()
         h_copy(1, side).wait_send()
-    pltpu.make_async_copy(v.at[0], out0, out_sem.at[0]).wait()
-    last.wait()
+    for upd in range(2):
+        for part in range(2):
+            result(upd, part).wait()
+
+
+def handed_out(in0, in1, out0, out1, sem, buf):
+    ins = [pltpu.make_async_copy(a, buf.at[i], sem.at[i]) for i, a in enumerate((in0, in1))]
+    outs = [pltpu.make_async_copy(buf.at[i], a, sem.at[i]) for i, a in enumerate((out0, out1))]
+    for copy in ins:
+        copy.start()
+    for i, o in zip(ins, outs):
+        i.wait()
+        o.start()
+    for copy in outs:
+        copy.wait()
 
 
 def on_device(nseg, nsec, *args):
     entries = float(nsec * BLK * DIM * DIM)
-    hbm = pl.BlockSpec(memory_space=pltpu.HBM)
+    hbm, anywhere = pl.BlockSpec(memory_space=pltpu.HBM), pl.BlockSpec(memory_space=pl.ANY)
     waves, envs = (BLK, DIM, DIM), (BLK, TERMS, DIM, DIM)
     dma = pltpu.SemaphoreType.DMA
     big = [a[0] for a in args[:8]]
@@ -338,7 +369,7 @@
         functools.partial(kernel, nseg, nsec, entries),
         out_shape=[jax.ShapeDtypeStruct(waves, F32)] * 2,
         in_specs=[hbm] * 10,
-        out_specs=[pl.BlockSpec(memory_space=pl.ANY)] * 2,
+        out_specs=[anywhere] * 2,
         scratch_shapes=[
             pltpu.VMEM((2, *waves), F32),
             pltpu.VMEM((2, *waves), F32),
@@ -367,13 +398,13 @@
             pltpu.SMEM((BLK, TERMS), jnp.int32),
             pltpu.SMEM((BLK,), jnp.int32),
             dma((10,)),
-            dma((2,)),
             dma((2, 2)),
             dma((2, 2)),
             dma((2, 2)),
             dma((2, 2)),
-            dma((BLK // PAIR, 2)),
-            dma((2, BLK // PAIR, 2)),
+            dma((2, 2)),
+            dma,
+            dma((2,)),
             dma,
             dma((2,)),
             dma((3,)),
@@ -387,6 +418,14 @@
         ),
         name="updates",
     )(*big, *args[8:])
+    outs = pl.pallas_call(
+        handed_out,
+        out_shape=[jax.ShapeDtypeStruct(waves, F32)] * 2,
+        in_specs=[anywhere] * 2,
+        out_specs=[hbm] * 2,
+        scratch_shapes=[dma((2,)), pltpu.VMEM((2, *waves), F32)],
+        name="results",
+    )(*outs)
     return tuple(o[None] for o in outs)
 
 

time: 84.4 us -> 80.4 us (0.953)
  local copies, waits for them, and re-layouts: 3.74 us -> 0 us
    unnamed x2 -> x0, local copies, waits for them, and re-layouts: 3.74 us -> none
    pallas_call x1, Pallas kernels: 79.8 us -> 77.6 us  [on_device(): pl.pallas_call(functools.partial(kernel, nseg, nsec, entries), out_shape=...]
    pallas_call x0 -> x1, Pallas kernels: none -> 2.02 us  [on_device(): pl.pallas_call(handed_out, out_shape=[jax.ShapeDtypeStruct(waves, F32)] *...]
where the time goes in v3:
time: 80.4 us; the launch traced here: 80.3 us
  Pallas kernels  79.6 us (99%)
    pallas_call x1, Pallas kernels, on_device(): pl.pallas_call(functools.partial(kernel, nseg, nsec, entries), out_shape=...  77.6 us
    pallas_call x1, Pallas kernels, on_device(): pl.pallas_call(handed_out, out_shape=[jax.ShapeDtypeStruct(waves, F32)] *...  2.02 us

profile of v3, /device:TPU:32, one launch (start us, length us, event | category | flops | bytes accessed | tf_op | source)
XLA Modules:
  0.0 80.3 jit_solution(7274597648485328817)
XLA Ops:
  0.6 77.6 %updates.1 = (f32[8,128,128]{2,1,0:T(8,128)}, f32[8,128,128]{2,1,0:T(8,128)}) custom-call(f32[8,128,128]{2,1,0:T(8,128)} %bitcast.14, f32[8,128,128]{2,1,0:T(8,128)} %bitcast.15, f32[8,128,128]{2,1,0:T(8,128)} %bitcast.16, f32[8,128,128]{2,1,0:T(8,128)} %bitcast.17, bf16[8,16,128,128]{3,2,1,0:T(8,128)(2,1)} %bitcast.10, bf16[8,16,128,128]{3,2,1,0:T(8,128)(2,1)} %bitcast.11, ...), custom_call_target="tpu_custom_call" | custom-call | flops 7516192768 | bytes 20971520 | tf_op jit(solution)/shard_map/updates/pallas_call | solution.py:368
  78.3 2.0 %results.1 = (f32[8,128,128]{2,1,0:T(8,128)}, f32[8,128,128]{2,1,0:T(8,128)}) custom-call(f32[8,128,128]{2,1,0:T(8,128)} %get-tuple-element.6.in0, f32[8,128,128]{2,1,0:T(8,128)} %get-tuple-element.7.in1), custom_call_target="tpu_custom_call" | custom-call | tf_op jit(solution)/shard_map/results/pallas_call | solution.py:421

commit v4 on v3

--- a/solution.py
+++ b/solution.py
@@ -138,14 +138,14 @@
     start_onsite(0)
     for i in range(4, 8):
         load(i).start()
+    for side in range(2):
+        v_copy(0, side).wait_send()
+    for side in range(2):
+        h_copy(0, side).start()
     load(4).wait()
     start_wave(1)
     load(5).wait()
     start_onsite(1)
-    for side in range(2):
-        v_copy(0, side).wait_send()
-    for side in range(2):
-        h_copy(0, side).start()
     for i in (9, 2, 3):
         load(i).wait()
 
@@ -249,6 +249,8 @@
             @pl.when(upd == 0)
             def _():
                 hand_copy(1).start()
+                for side in range(2):
+                    v_copy(1, side).start()
 
         r_all(par, r_rs.at[par]).wait()
         total = packet + jnp.sum(land_r[par], axis=0)
@@ -305,8 +307,6 @@
         r_all(par, r_ss).wait()
 
     def update(upd, _):
-        begin(upd)
-
         @pl.when(upd == 1)
         def _():
             load(6).wait()
@@ -315,6 +315,8 @@
             for i in range(3):
                 hand_copy(i).wait_send()
 
+        begin(upd)
+
         def each(it, _):
             step(upd, it, True)
             return 0
@@ -323,9 +325,6 @@
 
         @pl.when(upd == 0)
         def _():
-            for side in range(2):
-                v_copy(1, side).start()
-
             def one(b, _):
                 send_b[b] = (v[0, b] * hinv[0, b]).astype(BF16)
                 return 0

time: 80.4 us -> 80.7 us (level)
  no operation moved by 1% of the time
where the time goes in v4:
time: 80.7 us; the launch traced here: 80.6 us
  Pallas kernels  79.9 us (99%)
    pallas_call x1, Pallas kernels, on_device(): pl.pallas_call(functools.partial(kernel, nseg, nsec, entries), out_shape=...  77.9 us
    pallas_call x1, Pallas kernels, on_device(): pl.pallas_call(handed_out, out_shape=[jax.ShapeDtypeStruct(waves, F32)] *...  2.02 us

profile of v4, /device:TPU:32, one launch (start us, length us, event | category | flops | bytes accessed | tf_op | source)
XLA Modules:
  0.0 80.6 jit_solution(14844969324280724210)
XLA Ops:
  0.6 77.9 %updates.1 = (f32[8,128,128]{2,1,0:T(8,128)}, f32[8,128,128]{2,1,0:T(8,128)}) custom-call(f32[8,128,128]{2,1,0:T(8,128)} %bitcast.14, f32[8,128,128]{2,1,0:T(8,128)} %bitcast.15, f32[8,128,128]{2,1,0:T(8,128)} %bitcast.16, f32[8,128,128]{2,1,0:T(8,128)} %bitcast.17, bf16[8,16,128,128]{3,2,1,0:T(8,128)(2,1)} %bitcast.10, bf16[8,16,128,128]{3,2,1,0:T(8,128)(2,1)} %bitcast.11, ...), custom_call_target="tpu_custom_call" | custom-call | flops 7516192768 | bytes 20971520 | tf_op jit(solution)/shard_map/updates/pallas_call | solution.py:367
  78.6 2.0 %results.1 = (f32[8,128,128]{2,1,0:T(8,128)}, f32[8,128,128]{2,1,0:T(8,128)}) custom-call(f32[8,128,128]{2,1,0:T(8,128)} %get-tuple-element.6.in0, f32[8,128,128]{2,1,0:T(8,128)} %get-tuple-element.7.in1), custom_call_target="tpu_custom_call" | custom-call | tf_op jit(solution)/shard_map/results/pallas_call | solution.py:420

commit v5 on v4

--- a/solution.py
+++ b/solution.py
@@ -11,7 +11,7 @@
 BLK = 8
 TERMS = 16
 DIM = 128
-QUAD = 4
+QUAD = 8
 PAIR = 2
 MESH = pl.DeviceIdType.MESH
 F32, BF16 = jnp.float32, jnp.bfloat16
@@ -92,7 +92,7 @@
         )
 
     def result(upd, part):
-        rows = pl.ds(part * QUAD, QUAD)
+        rows = pl.ds(part * 4, 4)
         return pltpu.make_async_copy(v.at[upd, rows], (out0, out1)[upd].at[rows], out_sem.at[upd, part])
 
     def live(b):
@@ -210,13 +210,6 @@
                 if more and i % PAIR == PAIR - 1 and i < QUAD - 1:
                     for side in range(2):
                         a_copy(it, quad * (QUAD // PAIR) + i // PAIR, side).start()
-            if more:
-
-                @pl.when(quad == 0)
-                def _():
-                    for side in range(2):
-                        a_copy(it, QUAD // PAIR - 1, side).start()
-
             return 0
 
         lax.fori_loop(0, BLK // QUAD, quad_step, 0)
@@ -281,7 +274,7 @@
             lax.fori_loop(0, BLK, own, 0, unroll=4)
         else:
             for part in range(2):
-                lax.fori_loop(part * QUAD, (part + 1) * QUAD, own, 0, unroll=4)
+                lax.fori_loop(part * 4, (part + 1) * 4, own, 0, unroll=4)
 
                 @pl.when(upd == 0)
                 def _():
@@ -347,13 +340,20 @@
 
 
 def handed_out(in0, in1, out0, out1, sem, buf):
-    ins = [pltpu.make_async_copy(a, buf.at[i], sem.at[i]) for i, a in enumerate((in0, in1))]
-    outs = [pltpu.make_async_copy(buf.at[i], a, sem.at[i]) for i, a in enumerate((out0, out1))]
+    def parts(sources, targets):
+        return [
+            pltpu.make_async_copy(a.at[pl.ds(PAIR * j, PAIR)], b.at[pl.ds(PAIR * j, PAIR)], sem.at[i, j])
+            for i, (a, b) in enumerate(zip(sources, targets))
+            for j in range(BLK // PAIR)
+        ]
+
+    held = (buf.at[0], buf.at[1])
+    ins, outs = parts((in0, in1), held), parts(held, (out0, out1))
     for copy in ins:
         copy.start()
-    for i, o in zip(ins, outs):
-        i.wait()
-        o.start()
+    for arriving, leaving in zip(ins, outs):
+        arriving.wait()
+        leaving.start()
     for copy in outs:
         copy.wait()
 
@@ -422,7 +422,7 @@
         out_shape=[jax.ShapeDtypeStruct(waves, F32)] * 2,
         in_specs=[anywhere] * 2,
         out_specs=[hbm] * 2,
-        scratch_shapes=[dma((2,)), pltpu.VMEM((2, *waves), F32)],
+        scratch_shapes=[dma((2, BLK // PAIR)), pltpu.VMEM((2, *waves), F32)],
         name="results",
     )(*outs)
     return tuple(o[None] for o in outs)

time: 80.7 us -> 80.3 us (level)
  no operation moved by 1% of the time
where the time goes in v5:
time: 80.3 us; the launch traced here: 80.2 us
  Pallas kernels  79.5 us (99%)
    pallas_call x1, Pallas kernels, on_device(): pl.pallas_call(functools.partial(kernel, nseg, nsec, entries), out_shape=...  77.5 us
    pallas_call x1, Pallas kernels, on_device(): pl.pallas_call(handed_out, out_shape=[jax.ShapeDtypeStruct(waves, F32)] *...  2.02 us

profile of v5, /device:TPU:32, one launch (start us, length us, event | category | flops | bytes accessed | tf_op | source)
XLA Modules:
  0.0 80.2 jit_solution(9463415018519144959)
XLA Ops:
  0.6 77.5 %updates.1 = (f32[8,128,128]{2,1,0:T(8,128)}, f32[8,128,128]{2,1,0:T(8,128)}) custom-call(f32[8,128,128]{2,1,0:T(8,128)} %bitcast.14, f32[8,128,128]{2,1,0:T(8,128)} %bitcast.15, f32[8,128,128]{2,1,0:T(8,128)} %bitcast.16, f32[8,128,128]{2,1,0:T(8,128)} %bitcast.17, bf16[8,16,128,128]{3,2,1,0:T(8,128)(2,1)} %bitcast.10, bf16[8,16,128,128]{3,2,1,0:T(8,128)(2,1)} %bitcast.11, ...), custom_call_target="tpu_custom_call" | custom-call | flops 7516192768 | bytes 20971520 | tf_op jit(solution)/shard_map/updates/pallas_call | solution.py:367
  78.1 2.0 %results.1 = (f32[8,128,128]{2,1,0:T(8,128)}, f32[8,128,128]{2,1,0:T(8,128)}) custom-call(f32[8,128,128]{2,1,0:T(8,128)} %get-tuple-element.6.in0, f32[8,128,128]{2,1,0:T(8,128)} %get-tuple-element.7.in1), custom_call_target="tpu_custom_call" | custom-call | tf_op jit(solution)/shard_map/results/pallas_call | solution.py:420

commit v6 on v5

--- a/solution.py
+++ b/solution.py
@@ -101,7 +101,7 @@
         limit = dims[b]
         return (row < limit) & (col < limit)
 
-    for i in (0, 8, 1, 9, 2, 3):
+    for i in (0, 8):
         load(i).start()
 
     barrier = pltpu.get_barrier_semaphore()
@@ -134,6 +134,8 @@
     start_wave(0)
     for side in range(2):
         v_copy(0, side).start()
+    for i in (1, 9, 2, 3):
+        load(i).start()
     load(1).wait()
     start_onsite(0)
     for i in range(4, 8):

time: 80.3 us -> 80.3 us (level)
  no operation moved by 1% of the time
where the time goes in v6:
time: 80.3 us; the launch traced here: 80.2 us
  Pallas kernels  79.5 us (99%)
    pallas_call x1, Pallas kernels, on_device(): pl.pallas_call(functools.partial(kernel, nseg, nsec, entries), out_shape=...  77.5 us
    pallas_call x1, Pallas kernels, on_device(): pl.pallas_call(handed_out, out_shape=[jax.ShapeDtypeStruct(waves, F32)] *...  2.02 us

profile of v6, /device:TPU:32, one launch (start us, length us, event | category | flops | bytes accessed | tf_op | source)
XLA Modules:
  0.0 80.2 jit_solution(10229448887861389540)
XLA Ops:
  0.6 77.5 %updates.1 = (f32[8,128,128]{2,1,0:T(8,128)}, f32[8,128,128]{2,1,0:T(8,128)}) custom-call(f32[8,128,128]{2,1,0:T(8,128)} %bitcast.14, f32[8,128,128]{2,1,0:T(8,128)} %bitcast.15, f32[8,128,128]{2,1,0:T(8,128)} %bitcast.16, f32[8,128,128]{2,1,0:T(8,128)} %bitcast.17, bf16[8,16,128,128]{3,2,1,0:T(8,128)(2,1)} %bitcast.10, bf16[8,16,128,128]{3,2,1,0:T(8,128)(2,1)} %bitcast.11, ...), custom_call_target="tpu_custom_call" | custom-call | flops 7516192768 | bytes 20971520 | tf_op jit(solution)/shard_map/updates/pallas_call | solution.py:369
  78.2 2.0 %results.1 = (f32[8,128,128]{2,1,0:T(8,128)}, f32[8,128,128]{2,1,0:T(8,128)}) custom-call(f32[8,128,128]{2,1,0:T(8,128)} %get-tuple-element.6.in0, f32[8,128,128]{2,1,0:T(8,128)} %get-tuple-element.7.in1), custom_call_target="tpu_custom_call" | custom-call | tf_op jit(solution)/shard_map/results/pallas_call | solution.py:422
